TPU v7x, 32 devices: a whole 2x2x4 slice. The times are simulated.
32 devices in a mesh: slab: 16 (over z, y, x), tm: 2 (over core).
Axes of the slice: x: 2, y: 2, z: 4, core: 2. Of those that a mesh axis runs over, the one named last changes fastest.
Arguments:
- bold_series: bfloat16 [16, 262144], P('tm', 'slab'), may hold values from -6 to 6
- tile_index: int32 [2, 256], P(None, 'slab'), may hold values from 0 to 143, as said below
- ribbon_weight: bfloat16 [256, 256, 128], P(('slab', 'tm')), may hold values from -0.375 to 0.375
- vertex_area: bfloat16 [32768], P('slab'), may hold values from 0.25 to 4
- requests: int32 [16, 16, 768], P('slab'), may hold values from 0 to 2047
- corner_slot: int32 [3, 32768], P(None, 'slab'), may hold values from 0 to 12287, as said below
- barycentric: float32 [3, 32768], P(None, 'slab'), may hold values from 0.1 to 1
Outputs:
- fslr_series: float32 [16, 32768], P('tm', 'slab')
Inputs may be any that keep to these rules, and one draw needn't show every extreme that they name: `tile_index`: the tiles of vertex block g are 2 distinct values in [b * 8, b * 8 + 2 * 8 + 8) with b = g % 16. `corner_slot`: within the 2048 fsLR vertices of one patch, each slot serves at most one corner; the used slots of block set s are its first n slots, where n is 768 for a quarter of the block sets, 384 for half of them and 0 for the rest, and the patch uses exactly 6144 slots.
All inputs are finite; a program needn't handle non-finite values.
Results may differ from a plain program's by a relative error of at most 0.003.
Values may be sent and summed in bfloat16 or wider, within the bound.
A program may use at most 64 MiB of HBM per device.

v0:
```python
import jax
import jax.numpy as jnp
from jax import lax
from jax.sharding import PartitionSpec as P

HALO_T = 8


def extended_2(block, sides, width):
    for axis, dim in sides:
        count = lax.axis_size(axis)
        forward = [(i, i + 1) for i in range(count - 1)]
        backward = [(target, source) for source, target in forward]
        low = lax.ppermute(
            lax.slice_in_dim(block, block.shape[dim] - width, None, axis=dim), axis, forward
        )
        high = lax.ppermute(lax.slice_in_dim(block, 0, width, axis=dim), axis, backward)
        block = jnp.concatenate([low, block, high], axis=dim)
    return block


def sample_tiles(tile_rows, indices, weights):
    tile_len = weights.shape[2]
    blocks = indices.shape[1]
    picked = tile_rows[indices.T]
    shaped = weights.reshape(blocks, indices.shape[0], tile_len, tile_len)
    result = jnp.einsum("bkfu,bkuv->bvf", picked, shaped, preferred_element_type=jnp.float32)
    return result.reshape(blocks * tile_len, -1)


def shards(bold_series, tile_index, ribbon_weight, vertex_area, requests, corner_slot, barycentric):
    tile_len = ribbon_weight.shape[2]
    extended = extended_2(bold_series, (("slab", 1),), HALO_T * tile_len)
    frames = extended.shape[0]
    tile_rows = jnp.transpose(extended.reshape(frames, -1, tile_len), (1, 0, 2))
    native = sample_tiles(
        tile_rows, tile_index, lax.all_gather(ribbon_weight, "tm", axis=0, tiled=True)
    ).astype(jnp.bfloat16)
    fslr_count = corner_slot.shape[1]
    weighted = jnp.zeros((fslr_count, frames), jnp.float32)
    totals = jnp.zeros((fslr_count,), jnp.float32)
    wanted = lax.all_to_all(requests[0], "slab", split_axis=0, concat_axis=0, tiled=True)
    values = native[wanted]
    areas_row = vertex_area[wanted]
    got_values = lax.all_to_all(values, "slab", split_axis=0, concat_axis=0, tiled=True)
    got_areas = lax.all_to_all(areas_row, "slab", split_axis=0, concat_axis=0, tiled=True)
    flat_values = got_values.reshape(-1, frames)
    flat_areas = got_areas.reshape(-1)
    for which in range(3):
        column = corner_slot[which]
        factor = barycentric[which] * flat_areas[column].astype(jnp.float32)
        weighted = weighted + factor[:, None] * flat_values[column].astype(jnp.float32)
        totals = totals + factor
    return (weighted / totals[:, None]).T


def solution(mesh):
    placed = (
        P("tm", "slab"),
        P(None, "slab"),
        P(("slab", "tm"), None, None),
        P("slab"),
        P("slab", None, None),
        P(None, "slab"),
        P(None, "slab"),
    )
    return jax.shard_map(
        shards, mesh=mesh, in_specs=placed, out_specs=P("tm", "slab"), check_vma=False
    )
```

profile of v0, /device:TPU:0, one launch (start us, length us, event | category | flops | bytes accessed | tf_op | source)
XLA Modules:
  0.0 245.7 jit_solution(18166953622832772782)
XLA Ops:
  6.5 1.5 all_to_all.17
  8.0 8.3 %all-to-all-start = ((s32[16,1,768]{2,1,0:T(1,128)}), s32[16,1,768]{2,1,0:T(1,128)S(1)}, u32[]{:S(2)}, u32[]{:S(2)}) async-start(s32[16,1,768]{2,1,0:T(1,128)} %all_to_all.17), calls=%async_computation | async-start | bytes 98304 | tf_op jit(solution)/shard_map/all_to_all | solution.py:42
  16.4 0.7 fusion.2
  17.1 3.8 %collective-permute-start = (bf16[8,1024]{1,0:T(8,128)(2,1)S(1)}, bf16[8,1024]{1,0:T(8,128)(2,1)S(1)}, u32[]{:S(2)}, u32[]{:S(2)}) collective-permute-start(bf16[8,1024]{1,0:T(8,128)(2,1)S(1)} %get-tuple-element.9), channel_id=1, source_target_pairs={{0,2},{2,4},{4,6},{6,8},{8,10},{10,12},{12,14},{14,16},{16,18},{18... | collective-permute-start | bytes 49160 | tf_op jit(solution)/shard_map/ppermute | solution.py:14
  20.9 1.3 collective-permute-start.1
  22.3 0.9 compare_select_fusion.3
  23.2 0.9 fusion.3
  24.1 0.7 compare_select_fusion.4
  25.0 1.6 collective-permute-done.1
  26.6 1.0 maximum_bitcast_fusion
  27.5 0.6 gather_fusion.2
  28.2 75.8 %gather_fusion = bf16[12288]{0:T(1024)(128)(2,1)S(1)} fusion(bf16[2048]{0:T(1024)(128)(2,1)S(1)} %copy-done, s32[12288]{0:T(1024)S(1)} %broadcast_clamp_fusion), kind=kCustom, calls=%fused_computation | custom fusion | bytes 98304 | tf_op jit(solution)/shard_map/gather | solution.py:44
  104.1 0.5 broadcast.118
  104.6 0.8 reduce.1
  105.4 0.6 reshape.256
  106.0 7.3 %all-to-all-start.1 = ((bf16[16,2,384]{2,1,0:T(2,128)(2,1)}), bf16[16,2,384]{2,1,0:T(2,128)(2,1)S(1)}, u32[]{:S(2)}, u32[]{:S(2)}) async-start(bf16[16,2,384]{2,1,0:T(2,128)(2,1)} %reshape.256), calls=%async_computation.1 | async-start | bytes 49152 | tf_op jit(solution)/shard_map/all_to_all | solution.py:46
  113.4 1.5 fusion.1
  114.8 0.3 copy.21
  115.1 43.6 %gather_fusion.3 = bf16[12288,8]{1,0:T(8,128)(2,1)} fusion(bf16[2048,8]{1,0:T(8,128)(2,1)S(1)} %copy.21, s32[12288]{0:T(1024)S(1)} %broadcast_clamp_fusion), kind=kCustom, calls=%fused_computation.3 | custom fusion | bytes 442368 | tf_op jit(solution)/shard_map/gather | solution.py:43
  158.8 3.8 %copy.22 = bf16[16,768,8]{1,2,0:T(8,128)(2,1)} copy(bf16[16,768,8]{2,1,0:T(8,128)(2,1)} %bitcast.43) | data formatting | bytes 393216 | tf_op jit(solution)/shard_map/gather | solution.py:43
  162.5 6.9 %all-to-all-start.2 = ((bf16[16,768,8]{1,2,0:T(8,128)(2,1)}), bf16[16,768,8]{1,2,0:T(8,128)(2,1)S(1)}, u32[]{:S(2)}, u32[]{:S(2)}) async-start(bf16[16,768,8]{1,2,0:T(8,128)(2,1)} %copy.22), calls=%async_computation.2 | async-start | bytes 393216 | tf_op jit(solution)/shard_map/all_to_all | solution.py:45
  169.7 13.1 %gather_fusion.1 = bf16[2048]{0:T(1024)(128)(2,1)S(1)} fusion(bf16[12288]{0:T(1024)(128)(2,1)S(1)} %reshape.173, s32[2048]{0:T(1024)S(1)} %broadcast_clamp_fusion.3), kind=kCustom, calls=%fused_computation.1 | custom fusion | bytes 16384 | tf_op jit(solution)/shard_map/gather | solution.py:51
  182.8 13.1 %gather_fusion.5 = bf16[2048]{0:T(1024)(128)(2,1)S(1)} fusion(bf16[12288]{0:T(1024)(128)(2,1)S(1)} %reshape.173, s32[2048]{0:T(1024)S(1)} %broadcast_clamp_fusion.2), kind=kCustom, calls=%fused_computation.5 | custom fusion | bytes 16384 | tf_op jit(solution)/shard_map/gather | solution.py:51
  195.9 13.1 %gather_fusion.7 = bf16[2048]{0:T(1024)(128)(2,1)S(1)} fusion(bf16[12288]{0:T(1024)(128)(2,1)S(1)} %reshape.173, s32[2048]{0:T(1024)S(1)} %broadcast_clamp_fusion.1), kind=kCustom, calls=%fused_computation.7 | custom fusion | bytes 16384 | tf_op jit(solution)/shard_map/gather | solution.py:51
  209.0 1.5 copy.23
  210.5 8.0 %gather_fusion.4 = bf16[2048,8]{1,0:T(8,128)(2,1)} fusion(bf16[12288,8]{1,0:T(8,128)(2,1)S(1)} %bitcast.40, s32[2048]{0:T(1024)S(1)} %broadcast_clamp_fusion.3), kind=kCustom, calls=%fused_computation.4 | custom fusion | bytes 73728 | tf_op jit(solution)/shard_map/gather | solution.py:52
  218.5 8.0 %gather_fusion.6 = bf16[2048,8]{1,0:T(8,128)(2,1)} fusion(bf16[12288,8]{1,0:T(8,128)(2,1)S(1)} %bitcast.41, s32[2048]{0:T(1024)S(1)} %broadcast_clamp_fusion.2), kind=kCustom, calls=%fused_computation.6 | custom fusion | bytes 73728 | tf_op jit(solution)/shard_map/gather | solution.py:52
  226.5 8.0 %gather_fusion.8 = bf16[2048,8]{1,0:T(8,128)(2,1)} fusion(bf16[12288,8]{1,0:T(8,128)(2,1)S(1)} %bitcast.42, s32[2048]{0:T(1024)S(1)} %broadcast_clamp_fusion.1), kind=kCustom, calls=%fused_computation.8 | custom fusion | bytes 73728 | tf_op jit(solution)/shard_map/gather | solution.py:52
  234.5 1.2 copy.24
  235.8 1.2 copy.25
  237.0 1.2 copy.26
  238.2 0.7 divide_bitcast_fusion
  (22 shorter events, 0.6 us)
Async XLA Ops:
  6.5 21.7 %copy-start = (bf16[2048]{0:T(1024)(128)(2,1)S(1)}, bf16[2048]{0:T(1024)(128)(2,1)}, u32[]{:S(2)}) copy-start(bf16[2048]{0:T(1024)(128)(2,1)} %param.10) | copy-start | bytes 12292
  8.0 20.1 %all-to-all-start = ((s32[16,1,768]{2,1,0:T(1,128)}), s32[16,1,768]{2,1,0:T(1,128)S(1)}, u32[]{:S(2)}, u32[]{:S(2)}) async-start(s32[16,1,768]{2,1,0:T(1,128)} %all_to_all.17), calls=%async_computation | async-start | bytes 98304 | tf_op jit(solution)/shard_map/all_to_all | solution.py:42
  16.3 97.0 %all-gather.2.cloned.1.call-start = ((), (), s32[]{:S(2)}) async-start(), calls=%async_computation.3 | async-start | bytes 1572864 | tf_op jit(solution)/shard_map/all_gather | solution.py:37
  17.1 7.9 %collective-permute-start = (bf16[8,1024]{1,0:T(8,128)(2,1)S(1)}, bf16[8,1024]{1,0:T(8,128)(2,1)S(1)}, u32[]{:S(2)}, u32[]{:S(2)}) collective-permute-start(bf16[8,1024]{1,0:T(8,128)(2,1)S(1)} %get-tuple-element.9), channel_id=1, source_target_pairs={{0,2},{2,4},{4,6},{6,8},{8,10},{10,12},{12,14},{14,16},{16,18},{18... | collective-permute-start | bytes 49160 | tf_op jit(solution)/shard_map/ppermute | solution.py:14
  20.9 5.6 %collective-permute-start.1 = (bf16[8,1024]{1,0:T(8,128)(2,1)S(1)}, bf16[8,1024]{1,0:T(8,128)(2,1)S(1)}, u32[]{:S(2)}, u32[]{:S(2)}) collective-permute-start(bf16[8,1024]{1,0:T(8,128)(2,1)S(1)} %get-tuple-element.10), channel_id=1, source_target_pairs={{2,0},{4,2},{6,4},{8,6},{10,8},{12,10},{14,12},{16,14},{18,16},{20... | collective-permute-start | bytes 49160 | tf_op jit(solution)/shard_map/ppermute | solution.py:17
  106.0 56.5 %all-to-all-start.1 = ((bf16[16,2,384]{2,1,0:T(2,128)(2,1)}), bf16[16,2,384]{2,1,0:T(2,128)(2,1)S(1)}, u32[]{:S(2)}, u32[]{:S(2)}) async-start(bf16[16,2,384]{2,1,0:T(2,128)(2,1)} %reshape.256), calls=%async_computation.1 | async-start | bytes 49152 | tf_op jit(solution)/shard_map/all_to_all | solution.py:46
  162.5 46.4 %all-to-all-start.2 = ((bf16[16,768,8]{1,2,0:T(8,128)(2,1)}), bf16[16,768,8]{1,2,0:T(8,128)(2,1)S(1)}, u32[]{:S(2)}, u32[]{:S(2)}) async-start(bf16[16,768,8]{1,2,0:T(8,128)(2,1)} %copy.22), calls=%async_computation.2 | async-start | bytes 393216 | tf_op jit(solution)/shard_map/all_to_all | solution.py:45
Sparse Core Ops, SparseCore 0:
  22.4 11.0 all-gather.1
where the time goes:
time: 247 us; the launch traced here: 246 us
  local copies, waits for them, and re-layouts  197 us (80%)
  starting transfers between devices  27.7 us (11%)
  between operations  13.6 us (6%)
  other arithmetic  4.23 us (2%)
    gather x1, local copies, waits for them, and re-layouts, shards(): areas_row = vertex_area[wanted]  75.8 us
    gather x2, local copies, waits for them, and re-layouts, shards(): values = native[wanted]  47.4 us
    gather x3, local copies, waits for them, and re-layouts, shards(): factor = barycentric[which] * flat_areas[column].astype(jnp.float32)  39.2 us
    gather x6, local copies, waits for them, and re-layouts, shards(): flat_values[column].astype(jnp.float32)  27.7 us
    all_to_all x1, starting transfers between devices, shards(): lax.all_to_all(requests[0], 'slab', split_axis=0, concat_axis=0, tiled=True)  8.31 us
    all_to_all x1, starting transfers between devices, shards(): lax.all_to_all(areas_row, 'slab', split_axis=0, concat_axis=0, tiled=True)  7.35 us
    all_to_all x1, starting transfers between devices, shards(): lax.all_to_all(values, 'slab', split_axis=0, concat_axis=0, tiled=True)  6.9 us
  transfers between devices with their start and end apart: 6, of which 1 were waited for; matrix products, arithmetic and copies ran while one was open for 70% of the time, Pallas kernels for 0%

commit v1 on v0

v1 whole, which is shorter than its diff:
```python
import functools

import jax
import jax.numpy as jnp
from jax import lax
from jax.experimental import pallas as pl
from jax.experimental.pallas import tpu as pltpu
from jax.sharding import PartitionSpec as P

HALO_T = 8
LANES = 128
MESH = pl.DeviceIdType.MESH


def pick(table, lanes):
    return jnp.take_along_axis(table, lanes, axis=1, mode="promise_in_bounds")


def exchange_kernel(n, m, vregs, tidx, bold, w, area, req, vals, areas, ext, wall, nat, rq, out_buf,
                    halo_s, halo_r, w_s, w_r, rq_s, rq_r, ar_s, ar_r, va_s, va_r):
    me = lax.axis_index("slab")
    t = lax.axis_index("tm")
    tiles = bold.shape[1] // LANES
    own = w.shape[0]
    frames = bold.shape[0]
    blocks = nat.shape[0]
    half = vregs // 2
    halo = HALO_T

    barrier = pltpu.get_barrier_semaphore()

    @pl.loop(1, n)
    def _(r):
        pl.semaphore_signal(barrier, inc=1, device_id={"slab": lax.rem(me + r, n)}, device_id_type=MESH)

    for q in range(1, m):
        pl.semaphore_signal(barrier, inc=1, device_id={"tm": lax.rem(t + q, m)}, device_id_type=MESH)

    def widen(lo, hi):
        for i in range(lo, hi):
            ext[halo + i] = bold[:, i * LANES:(i + 1) * LANES].astype(jnp.float32)

    widen(0, halo)
    widen(tiles - halo, tiles)

    @pl.when(me == 0)
    def _():
        ext[0:halo] = jnp.zeros((halo, frames, LANES), jnp.float32)

    @pl.when(me == n - 1)
    def _():
        ext[halo + tiles:] = jnp.zeros((halo, frames, LANES), jnp.float32)

    pl.semaphore_wait(barrier, n - 1 + m - 1)

    to_right = pltpu.make_async_remote_copy(
        src_ref=ext.at[pl.ds(tiles, halo)], dst_ref=ext.at[pl.ds(0, halo)],
        send_sem=halo_s.at[0], recv_sem=halo_r.at[0],
        device_id={"slab": lax.rem(me + 1, n)}, device_id_type=MESH)
    to_left = pltpu.make_async_remote_copy(
        src_ref=ext.at[pl.ds(halo, halo)], dst_ref=ext.at[pl.ds(halo + tiles, halo)],
        send_sem=halo_s.at[1], recv_sem=halo_r.at[1],
        device_id={"slab": lax.rem(me + n - 1, n)}, device_id_type=MESH)

    @pl.when(me < n - 1)
    def _():
        to_right.start()

    @pl.when(me > 0)
    def _():
        to_left.start()

    def weights_copy(q, owner):
        return pltpu.make_async_remote_copy(
            src_ref=w, dst_ref=wall.at[pl.ds(owner * own, own)],
            send_sem=w_s.at[q], recv_sem=w_r.at[q],
            device_id={"tm": lax.rem(t + q, m)}, device_id_type=MESH)

    for q in range(1, m):
        weights_copy(q, t).start()

    def request_copy(r, to, slot):
        return pltpu.make_async_remote_copy(
            src_ref=req.at[to], dst_ref=rq.at[slot], send_sem=rq_s.at[r], recv_sem=rq_r.at[r],
            device_id={"slab": to}, device_id_type=MESH)

    def area_copy(r, to, slot):
        return pltpu.make_async_remote_copy(
            src_ref=area, dst_ref=areas.at[slot], send_sem=ar_s.at[r], recv_sem=ar_r.at[r],
            device_id={"slab": to}, device_id_type=MESH)

    def value_copy(r, to, slot):
        return pltpu.make_async_remote_copy(
            src_ref=out_buf.at[to], dst_ref=vals.at[slot], send_sem=va_s.at[r], recv_sem=va_r.at[r],
            device_id={"slab": to}, device_id_type=MESH)

    @pl.loop(1, n)
    def _(r):
        request_copy(r, lax.rem(me + r, n), me).start()

    @pl.loop(1, n)
    def _(r):
        area_copy(r, lax.rem(me + r, n), me).start()

    widen(halo, tiles - halo)
    areas[me] = area[...]

    @pl.when(me > 0)
    def _():
        to_right.wait_recv()

    @pl.when(me < n - 1)
    def _():
        to_left.wait_recv()

    def native_block(block, weights):
        x = jnp.concatenate([ext[tidx[k, block]] for k in range(2)], axis=1).astype(jnp.bfloat16)
        y = jnp.dot(x, weights, preferred_element_type=jnp.float32)
        nat[block] = y.astype(jnp.bfloat16).astype(jnp.float32)

    for i in range(own):
        native_block(t * own + i, w[i])
    for q in range(1, m):
        owner = lax.rem(t + m - q, m)
        weights_copy(q, owner).wait_recv()
        for i in range(own):
            native_block(owner * own + i, wall[owner * own + i])

    table = [nat[h] for h in range(blocks)]

    def selected(wanted):
        found = []
        for v in range(vregs):
            row = jnp.broadcast_to(wanted[v:v + 1], (frames, LANES))
            lo, hi = row & (LANES - 1), row >> 7
            acc = pick(table[0], lo)
            for h in range(1, blocks):
                acc = jnp.where(hi == h, pick(table[h], lo), acc)
            found.append(acc)
        return [jnp.concatenate([found[v], found[half + v]], axis=0).astype(jnp.bfloat16) for v in range(half)]

    @pl.loop(1, n)
    def _(r):
        to = lax.rem(me + r, n)
        request_copy(n - r, to, to).wait_recv()
        for v, piece in enumerate(selected(rq[to])):
            out_buf[to, :, v * LANES:(v + 1) * LANES] = piece
        value_copy(r, to, me).start()

    for v, piece in enumerate(selected(req[me])):
        vals[me, :, v * LANES:(v + 1) * LANES] = piece

    @pl.loop(1, n)
    def _(r):
        source = lax.rem(me + n - r, n)
        area_copy(r, source, source).wait_recv()
        value_copy(r, source, source).wait_recv()

    @pl.loop(1, n)
    def _(r):
        to = lax.rem(me + r, n)
        request_copy(r, to, me).wait_send()
        area_copy(r, to, me).wait_send()
        value_copy(r, to, me).wait_send()

    for q in range(1, m):
        weights_copy(q, t).wait_send()

    @pl.when(me < n - 1)
    def _():
        to_right.wait_send()

    @pl.when(me > 0)
    def _():
        to_left.wait_send()


def corners_kernel(cap, vregs, vals, areas, req, slot, bary, out, tbl, area_at, lo_ref, hi_ref, fac):
    n = vals.shape[0]
    rows = areas.shape[1]
    half = vregs // 2
    for s in range(n):
        for v in range(half):
            both = vals[s, :, v * LANES:(v + 1) * LANES].astype(jnp.float32)
            tbl[s * vregs + v] = both[:8]
            tbl[s * vregs + half + v] = both[8:]

    @pl.loop(0, n)
    def _(s):
        wanted = req[s]
        lo, hi = wanted & (LANES - 1), wanted >> 7
        a = areas[s].astype(jnp.float32)
        acc = jnp.zeros((8, LANES), jnp.float32)
        for h in range(rows):
            acc = jnp.where(hi == h, pick(jnp.broadcast_to(a[h:h + 1], (8, LANES)), lo), acc)
        area_at[s] = acc

    flat = slot[...]
    if cap % LANES == 0 and cap == vregs * LANES:
        lo_ref[...] = flat & (LANES - 1)
        hi_ref[...] = flat >> 7
    else:
        source = ((flat.astype(jnp.float32) + 0.5) * (1.0 / cap)).astype(jnp.int32)
        rest = flat - source * cap
        lo_ref[...] = rest & (LANES - 1)
        hi_ref[...] = source * vregs + (rest >> 7)

    @pl.loop(0, slot.shape[0] // 8)
    def _(b):
        at = pl.ds(pl.multiple_of(b * 8, 8), 8)
        lo, hi = lo_ref[at], hi_ref[at]
        acc = jnp.zeros((8, LANES), jnp.float32)
        for s in range(n):
            found = area_at[s]
            for v in range(vregs):
                row = jnp.broadcast_to(found[v:v + 1], (8, LANES))
                acc = jnp.where(hi == s * vregs + v, pick(row, lo), acc)
        fac[at] = bary[at] * acc

    per = slot.shape[0] // 3

    @pl.loop(0, per)
    def _(g):
        lo = [jnp.broadcast_to(lo_ref[pl.ds(k * per + g, 1)], (8, LANES)) for k in range(3)]
        hi = [jnp.broadcast_to(hi_ref[pl.ds(k * per + g, 1)], (8, LANES)) for k in range(3)]
        f = [fac[pl.ds(k * per + g, 1)] for k in range(3)]
        acc = [jnp.zeros((8, LANES), jnp.float32)] * 3
        for e in range(n * vregs):
            here = tbl[e]
            for k in range(3):
                acc[k] = jnp.where(hi[k] == e, pick(here, lo[k]), acc[k])
        top = sum(jnp.broadcast_to(f[k], (8, LANES)) * acc[k] for k in range(3))
        total = jnp.broadcast_to(f[0] + f[1] + f[2], (8, LANES))
        out[:, pl.ds(pl.multiple_of(g * LANES, LANES), LANES)] = top / total


def shards(bold, tile_index, weights, area, requests, slot, bary):
    n, m = lax.axis_size("slab"), lax.axis_size("tm")
    frames = bold.shape[0]
    cap = requests.shape[2]
    vregs = 2 * (-(-cap // (2 * LANES)))
    own, depth, tile = weights.shape
    blocks = own * m
    vmem = pl.BlockSpec(memory_space=pltpu.VMEM)
    smem = pl.BlockSpec(memory_space=pltpu.SMEM)
    req = jnp.pad(requests[0], ((0, 0), (0, 8 * LANES - cap))).reshape(n, 8, LANES)
    sem = lambda k: pltpu.SemaphoreType.DMA((k,))
    vals, areas = pl.pallas_call(
        functools.partial(exchange_kernel, n, m, vregs),
        out_shape=(
            jax.ShapeDtypeStruct((n, 2 * frames, vregs // 2 * LANES), jnp.bfloat16),
            jax.ShapeDtypeStruct((n, area.shape[0] // LANES, LANES), jnp.bfloat16),
        ),
        in_specs=[smem, vmem, vmem, vmem, vmem],
        out_specs=(vmem, vmem),
        scratch_shapes=[
            pltpu.VMEM((bold.shape[1] // LANES + 2 * HALO_T, frames, LANES), jnp.float32),
            pltpu.VMEM((blocks, depth, tile), jnp.bfloat16),
            pltpu.VMEM((blocks, frames, LANES), jnp.float32),
            pltpu.VMEM((n, 8, LANES), jnp.int32),
            pltpu.VMEM((n, 2 * frames, vregs // 2 * LANES), jnp.bfloat16),
            sem(2), sem(2), sem(m), sem(m), sem(n), sem(n), sem(n), sem(n), sem(n), sem(n),
        ],
        compiler_params=pltpu.CompilerParams(
            collective_id=0, has_side_effects=True, vmem_limit_bytes=24 * 2 ** 20),
        name="exchange",
    )(tile_index, bold, weights, area.reshape(-1, LANES), req)
    rows = 3 * slot.shape[1] // LANES
    return pl.pallas_call(
        functools.partial(corners_kernel, cap, vregs),
        out_shape=jax.ShapeDtypeStruct((frames, slot.shape[1]), jnp.float32),
        in_specs=[vmem] * 5,
        out_specs=vmem,
        scratch_shapes=[
            pltpu.VMEM((n * vregs, 8, LANES), jnp.float32),
            pltpu.VMEM((n, 8, LANES), jnp.float32),
            pltpu.VMEM((rows, LANES), jnp.int32),
            pltpu.VMEM((rows, LANES), jnp.int32),
            pltpu.VMEM((rows, LANES), jnp.float32),
        ],
        compiler_params=pltpu.CompilerParams(vmem_limit_bytes=24 * 2 ** 20),
        name="corners",
    )(vals, areas, req, slot.reshape(rows, LANES), bary.reshape(rows, LANES))


def solution(mesh):
    placed = (
        P("tm", "slab"),
        P(None, "slab"),
        P(("slab", "tm"), None, None),
        P("slab"),
        P("slab", None, None),
        P(None, "slab"),
        P(None, "slab"),
    )
    return jax.shard_map(
        shards, mesh=mesh, in_specs=placed, out_specs=P("tm", "slab"), check_vma=False
    )
```

time: 247 us -> 38.2 us (0.15)
  local copies, waits for them, and re-layouts: 197 us -> 3.37 us
  Pallas kernels: 0 us -> 34.5 us
  starting transfers between devices: 27.7 us -> 0 us
  between operations: 13.6 us -> 0.05 us
  other arithmetic: 4.23 us -> 0 us
    gather x13 -> x0, local copies, waits for them, and re-layouts: 191 us -> none  [the longest x1 75.8 us: shards(): areas_row = vertex_area[wanted]]
    pallas_call x0 -> x2, Pallas kernels: none -> 34.5 us  [the longest x1 18.7 us: shards(): pl.pallas_call(functools.partial(exchange_kernel, n, m, vregs), out_shape...]
    all_to_all x3 -> x0, starting transfers between devices: 22.6 us -> none  [the longest x1 8.31 us: shards(): lax.all_to_all(requests[0], 'slab', split_axis=0, concat_axis=0, tiled=True)]
    ppermute x2 -> x0, starting transfers between devices: 5.11 us -> none  [the longest x1 3.81 us: extended_2(): lax.ppermute(lax.slice_in_dim(block, block.shape[dim] - width, None, axis...]
    all_to_all x4 -> x0, local copies, waits for them, and re-layouts: 3.49 us -> none  [the longest x1 1.5 us: shards(): lax.all_to_all(values, 'slab', split_axis=0, concat_axis=0, tiled=True)]
  transfers between devices with their start and end apart: 6 -> 0, of which waited for: 1 -> 0; matrix products, arithmetic and copies ran while one was open for 70% -> 0% of each run, Pallas kernels for 0% -> 0%
where the time goes in v1:
time: 38.2 us; the launch traced here: 37.9 us
  Pallas kernels  34.5 us (90%)
  local copies, waits for them, and re-layouts  3.37 us (9%)
    pallas_call x1, Pallas kernels, shards(): pl.pallas_call(functools.partial(exchange_kernel, n, m, vregs), out_shape...  18.7 us
    pallas_call x1, Pallas kernels, shards(): pl.pallas_call(functools.partial(corners_kernel, cap, vregs), out_shape=j...  15.8 us
    unnamed x12, local copies, waits for them, and re-layouts  2.53 us
    reshape x1, local copies, waits for them, and re-layouts, shards(): slot.reshape(rows, LANES)  0.82 us

profile of v1, /device:TPU:0, one launch (start us, length us, event | category | flops | bytes accessed | tf_op | source)
XLA Modules:
  0.0 37.9 jit_solution(11785640978975397161)
XLA Ops:
  0.0 0.0 copy-start.4
  0.0 0.0 copy-start.1
  0.0 0.8 %reshape.14.slot = s32[48,128]{1,0:T(8,128)S(1)} reshape(s32[3,2048]{1,0:T(4,128)} %param.12) | data formatting | bytes 49152 | tf_op jit(solution)/shard_map/reshape | solution.py:283
  0.8 0.0 copy-done.4
  0.9 0.8 %pad_bitcast_fusion = s32[2,8,8,128]{3,1,2,0:T(8,128)S(1)} fusion(s32[16,768]{1,0:T(8,128)} %bitcast.8), kind=kLoop, calls=%fused_computation | loop fusion | bytes 114688
  1.7 0.0 copy-start.2
  1.7 0.0 copy-start.3
  1.7 0.0 copy-done.1
  1.7 0.6 %copy-done.2 = bf16[2048]{0:T(1024)(128)(2,1)S(1)} copy-done((bf16[2048]{0:T(1024)(128)(2,1)S(1)}, bf16[2048]{0:T(1024)(128)(2,1)}, u32[]{:S(2)}) %copy-start.2) | copy-done | bytes 4120
  2.4 0.0 copy-done.3
  2.4 0.0 copy-start
  2.4 1.0 %copy-done = bf16[8,256,128]{2,1,0:T(8,128)(2,1)S(1)} copy-done((bf16[8,256,128]{2,1,0:T(8,128)(2,1)S(1)}, bf16[8,256,128]{2,1,0:T(8,128)(2,1)}, u32[]{:S(2)}) %copy-start) | copy-done | bytes 524312
  3.4 18.7 %exchange.1 = (bf16[16,16,384]{2,1,0:T(8,128)(2,1)S(1)}, bf16[16,16,128]{2,1,0:T(8,128)(2,1)S(1)}) custom-call(s32[2,16]{1,0:T(2,128)S(1)} %copy-done.3, bf16[8,16384]{1,0:T(8,128)(2,1)S(1)} %copy-done.1, bf16[8,256,128]{2,1,0:T(8,128)(2,1)S(1)} %copy-done, bf16[16,128]{1,0:T(8,128)(2,1)S(1)} %bitcast.7, s32[16,8,128]{2,1,0:T(8,128)S(1)} %bitcast.5), custom_call_target="tpu_custom_call" | custom-call | tf_op jit(solution)/shard_map/exchange/pallas_call | solution.py:248
  22.1 15.8 %corners.1 = f32[8,2048]{1,0:T(8,128)} custom-call(bf16[16,16,384]{2,1,0:T(8,128)(2,1)S(1)} %get-tuple-element.7.vals, bf16[16,16,128]{2,1,0:T(8,128)(2,1)S(1)} %get-tuple-element.8.areas, s32[16,8,128]{2,1,0:T(8,128)S(1)} %bitcast.6, s32[48,128]{1,0:T(8,128)S(1)} %reshape.14.slot, f32[48,128]{1,0:T(8,128)S(1)} %reshape.15.bary), custom_call_target="tpu_custom_call" | custom-call | tf_op jit(solution)/shard_map/corners/pallas_call | solution.py:269
  (2 shorter events, 0.0 us)
Async XLA Ops:
  0.0 0.8 %copy-start.4 = (f32[3,2048]{1,0:T(4,128)S(1)}, f32[3,2048]{1,0:T(4,128)}, u32[]{:S(2)}) copy-start(f32[3,2048]{1,0:T(4,128)} %param.13) | copy-start | bytes 73732
  0.0 1.7 %copy-start.1 = (bf16[8,16384]{1,0:T(8,128)(2,1)S(1)}, bf16[8,16384]{1,0:T(8,128)(2,1)}, u32[]{:S(2)}) copy-start(bf16[8,16384]{1,0:T(8,128)(2,1)} %bold.1) | copy-start | bytes 786436
  1.7 0.7 %copy-start.2 = (bf16[2048]{0:T(1024)(128)(2,1)S(1)}, bf16[2048]{0:T(1024)(128)(2,1)}, u32[]{:S(2)}) copy-start(bf16[2048]{0:T(1024)(128)(2,1)} %param.10) | copy-start | bytes 12292
  1.7 0.7 %copy-start.3 = (s32[2,16]{1,0:T(2,128)S(1)}, s32[2,16]{1,0:T(2,128)}, u32[]{:S(2)}) copy-start(s32[2,16]{1,0:T(2,128)} %tidx.1) | copy-start | bytes 388
  2.4 1.0 %copy-start = (bf16[8,256,128]{2,1,0:T(8,128)(2,1)S(1)}, bf16[8,256,128]{2,1,0:T(8,128)(2,1)}, u32[]{:S(2)}) copy-start(bf16[8,256,128]{2,1,0:T(8,128)(2,1)} %w.1) | copy-start | bytes 1572868

commit v2 on v1

v2 whole, which is shorter than its diff:
```python
import functools

import jax
import jax.numpy as jnp
from jax import lax
from jax.experimental import pallas as pl
from jax.experimental.pallas import tpu as pltpu
from jax.sharding import PartitionSpec as P

HALO_T = 8
LANES = 128
MESH = pl.DeviceIdType.MESH


def pick(table, lanes):
    return jnp.take_along_axis(table, lanes, axis=1, mode="promise_in_bounds")


def one_hot(lo):
    rows = lax.broadcasted_iota(jnp.int32, (LANES, lo.shape[1]), 0)
    return jnp.where(rows == lo, 1.0, 0.0).astype(jnp.bfloat16)


def exchange_kernel(n, m, vregs, tidx, bold_in, w, area, wanted_in, vals, area_at, ext, wall, nat, req, rq, areas, out_buf,
                    bold, wanted, in_s, halo_s, halo_r, w_s, w_r, rq_s, rq_r, ar_s, ar_r, va_s, va_r):
    me = lax.axis_index("slab")
    t = lax.axis_index("tm")
    tiles = bold.shape[1] // LANES
    own = w.shape[0]
    frames = bold.shape[0]
    blocks = nat.shape[0]
    half = vregs // 2
    halo = HALO_T
    cap = wanted.shape[1]

    load_bold = pltpu.make_async_copy(bold_in, bold, in_s.at[0])
    load_wanted = pltpu.make_async_copy(wanted_in, wanted, in_s.at[1])
    load_area = pltpu.make_async_copy(area, areas.at[me], in_s.at[2])
    mine = pltpu.make_async_copy(w, wall.at[pl.ds(t * own, own)], w_s.at[0])
    load_bold.start()
    load_wanted.start()
    load_area.start()
    mine.start()
    barrier = pltpu.get_barrier_semaphore()

    @pl.loop(1, n)
    def _(r):
        pl.semaphore_signal(barrier, inc=1, device_id={"slab": lax.rem(me + r, n)}, device_id_type=MESH)

    for q in range(1, m):
        pl.semaphore_signal(barrier, inc=1, device_id={"tm": lax.rem(t + q, m)}, device_id_type=MESH)

    load_bold.wait()

    def widen(lo, hi):
        for i in range(lo, hi):
            ext[halo + i] = bold[:, i * LANES:(i + 1) * LANES].astype(jnp.float32)

    widen(0, halo)
    widen(tiles - halo, tiles)

    @pl.when(me == 0)
    def _():
        ext[0:halo] = jnp.zeros((halo, frames, LANES), jnp.float32)

    @pl.when(me == n - 1)
    def _():
        ext[halo + tiles:] = jnp.zeros((halo, frames, LANES), jnp.float32)

    load_wanted.wait()
    req[...] = jnp.zeros(req.shape, jnp.int32)
    for s in range(n):
        for v in range(vregs):
            size = min(LANES, cap - v * LANES)
            if size > 0:
                req[s, v:v + 1, 0:size] = wanted[s:s + 1, v * LANES:v * LANES + size]

    pl.semaphore_wait(barrier, n - 1 + m - 1)

    def weights_copy(q, owner):
        return pltpu.make_async_remote_copy(
            src_ref=w, dst_ref=wall.at[pl.ds(owner * own, own)],
            send_sem=w_s.at[q], recv_sem=w_r.at[q],
            device_id={"tm": lax.rem(t + q, m)}, device_id_type=MESH)

    for q in range(1, m):
        weights_copy(q, t).start()

    to_right = pltpu.make_async_remote_copy(
        src_ref=ext.at[pl.ds(tiles, halo)], dst_ref=ext.at[pl.ds(0, halo)],
        send_sem=halo_s.at[0], recv_sem=halo_r.at[0],
        device_id={"slab": lax.rem(me + 1, n)}, device_id_type=MESH)
    to_left = pltpu.make_async_remote_copy(
        src_ref=ext.at[pl.ds(halo, halo)], dst_ref=ext.at[pl.ds(halo + tiles, halo)],
        send_sem=halo_s.at[1], recv_sem=halo_r.at[1],
        device_id={"slab": lax.rem(me + n - 1, n)}, device_id_type=MESH)

    @pl.when(me < n - 1)
    def _():
        to_right.start()

    @pl.when(me > 0)
    def _():
        to_left.start()

    def request_copy(r, to, slot):
        return pltpu.make_async_remote_copy(
            src_ref=req.at[to], dst_ref=rq.at[slot], send_sem=rq_s.at[r], recv_sem=rq_r.at[r],
            device_id={"slab": to}, device_id_type=MESH)

    def area_copy(r, to, slot):
        return pltpu.make_async_remote_copy(
            src_ref=area, dst_ref=areas.at[slot], send_sem=ar_s.at[r], recv_sem=ar_r.at[r],
            device_id={"slab": to}, device_id_type=MESH)

    def value_copy(r, to, slot):
        return pltpu.make_async_remote_copy(
            src_ref=out_buf.at[to], dst_ref=vals.at[slot], send_sem=va_s.at[r], recv_sem=va_r.at[r],
            device_id={"slab": to}, device_id_type=MESH)

    @pl.loop(1, n)
    def _(r):
        request_copy(r, lax.rem(me + r, n), me).start()

    @pl.loop(1, n)
    def _(r):
        area_copy(r, lax.rem(me + r, n), me).start()

    widen(halo, tiles - halo)
    load_area.wait()
    mine.wait()

    @pl.when(me > 0)
    def _():
        to_right.wait_recv()

    @pl.when(me < n - 1)
    def _():
        to_left.wait_recv()

    for q in range(m):
        owner = lax.rem(t + m - q, m)
        if q:
            weights_copy(q, owner).wait_recv()
        for i in range(own):
            block = owner * own + i
            x = jnp.concatenate([ext[tidx[k, block]] for k in range(2)], axis=1).astype(jnp.bfloat16)
            nat[block] = jnp.dot(x, wall[block], preferred_element_type=jnp.float32)

    table = nat[...].reshape(blocks * frames, LANES).astype(jnp.bfloat16)

    def selected(rows, put):
        for v in range(half):
            row = jnp.concatenate([rows[v:v + 1], rows[half + v:half + v + 1]], axis=1)
            lo = row & (LANES - 1)
            hi = jnp.broadcast_to(row >> 7, (frames, 2 * LANES))
            found = jnp.dot(table, one_hot(lo), preferred_element_type=jnp.float32)
            acc = found[:frames]
            for h in range(1, blocks):
                acc = jnp.where(hi == h, found[h * frames:(h + 1) * frames], acc)
            put(v, jnp.concatenate([acc[:, :LANES], acc[:, LANES:]], axis=0).astype(jnp.bfloat16))

    @pl.loop(1, n)
    def _(r):
        to = lax.rem(me + r, n)
        request_copy(n - r, to, to).wait_recv()

        def put(v, piece):
            out_buf[to, v * 16:(v + 1) * 16, :] = piece

        selected(rq[to], put)
        value_copy(r, to, me).start()

    def put_own(v, piece):
        vals[me, v * 16:(v + 1) * 16, :] = piece

    selected(req[me], put_own)

    @pl.loop(1, n)
    def _(r):
        source = lax.rem(me + n - r, n)
        area_copy(r, source, source).wait_recv()

    @pl.loop(0, n)
    def _(s):
        rows = req[s]
        lo, hi = rows & (LANES - 1), rows >> 7
        a = areas[s].astype(jnp.float32)
        acc = jnp.zeros((8, LANES), jnp.float32)
        for h in range(blocks):
            acc = jnp.where(hi == h, pick(jnp.broadcast_to(a[h:h + 1], (8, LANES)), lo), acc)
        area_at[s] = acc

    @pl.loop(1, n)
    def _(r):
        source = lax.rem(me + n - r, n)
        value_copy(r, source, source).wait_recv()

    @pl.loop(1, n)
    def _(r):
        to = lax.rem(me + r, n)
        request_copy(r, to, me).wait_send()
        area_copy(r, to, me).wait_send()
        value_copy(r, to, me).wait_send()

    for q in range(1, m):
        weights_copy(q, t).wait_send()

    @pl.when(me < n - 1)
    def _():
        to_right.wait_send()

    @pl.when(me > 0)
    def _():
        to_left.wait_send()


def corners_kernel(cap, vregs, vals, area_at, slot, bary, out, tbl, packed):
    n = area_at.shape[0]
    half = vregs // 2
    frames = out.shape[0]
    entries = n * vregs
    width = 2 * LANES
    tbl[:entries * frames] = vals[...]
    for s in range(n):
        packed[s * vregs:(s + 1) * vregs] = area_at[s, :vregs]
    tbl[entries * frames:] = packed[...].astype(jnp.bfloat16)

    @pl.loop(0, out.shape[1] // width)
    def _(g):
        at = pl.ds(pl.multiple_of(g * width, width), width)
        top = jnp.zeros((frames, width), jnp.float32)
        total = jnp.zeros((1, width), jnp.float32)
        for k in range(3):
            flat = slot[k:k + 1, at]
            if cap == vregs * LANES:
                lo, hi = flat & (LANES - 1), flat >> 7
            else:
                source = ((flat.astype(jnp.float32) + 0.5) * (1.0 / cap)).astype(jnp.int32)
                rest = flat - source * cap
                lo, hi = rest & (LANES - 1), source * vregs + (rest >> 7)
            found = jnp.dot(tbl[...], one_hot(lo), preferred_element_type=jnp.float32)
            wide = jnp.broadcast_to(hi, (frames, width))
            acc = jnp.zeros((frames, width), jnp.float32)
            for s in range(n):
                for v in range(half):
                    for j in range(2):
                        e = (s * half + v) * 2 + j
                        here = found[e * frames:(e + 1) * frames]
                        acc = jnp.where(wide == s * vregs + j * half + v, here, acc)
            row8 = lax.broadcasted_iota(jnp.int32, (8, width), 0)
            spread = jnp.zeros((8, width), jnp.float32)
            for b in range(entries // 8):
                at8 = entries * frames + b * 8
                spread = jnp.where(wide == row8 + b * 8, found[at8:at8 + 8], spread)
            factor = bary[k:k + 1, at] * jnp.sum(spread, axis=0, keepdims=True)
            top = top + factor * acc
            total = total + factor
        out[:, at] = top / total


def shards(bold, tile_index, weights, area, requests, slot, bary):
    n, m = lax.axis_size("slab"), lax.axis_size("tm")
    frames = bold.shape[0]
    cap = requests.shape[2]
    vregs = 2 * (-(-cap // (2 * LANES)))
    own, depth, tile = weights.shape
    blocks = own * m
    message = vregs * frames
    entries = n * vregs
    vmem = pl.BlockSpec(memory_space=pltpu.VMEM)
    hbm = pl.BlockSpec(memory_space=pltpu.HBM)
    smem = pl.BlockSpec(memory_space=pltpu.SMEM)
    sem = lambda k: pltpu.SemaphoreType.DMA((k,))
    vals, area_at = pl.pallas_call(
        functools.partial(exchange_kernel, n, m, vregs),
        out_shape=(
            jax.ShapeDtypeStruct((n, message, LANES), jnp.bfloat16),
            jax.ShapeDtypeStruct((n, 8, LANES), jnp.float32),
        ),
        in_specs=[smem, hbm, hbm, hbm, hbm],
        out_specs=(vmem, vmem),
        scratch_shapes=[
            pltpu.VMEM((bold.shape[1] // LANES + 2 * HALO_T, frames, LANES), jnp.float32),
            pltpu.VMEM((blocks, depth, tile), jnp.bfloat16),
            pltpu.VMEM((blocks, frames, LANES), jnp.float32),
            pltpu.VMEM((n, 8, LANES), jnp.int32),
            pltpu.VMEM((n, 8, LANES), jnp.int32),
            pltpu.VMEM((n, area.shape[0] // LANES, LANES), jnp.bfloat16),
            pltpu.VMEM((n, message, LANES), jnp.bfloat16),
            pltpu.VMEM(bold.shape, jnp.bfloat16),
            pltpu.VMEM((n, cap), jnp.int32),
            sem(3), sem(2), sem(2), sem(m), sem(m), sem(n), sem(n), sem(n), sem(n), sem(n), sem(n),
        ],
        compiler_params=pltpu.CompilerParams(
            collective_id=0, has_side_effects=True),
        name="exchange",
    )(tile_index, bold, weights, area.reshape(-1, LANES), requests.reshape(n, cap))
    return pl.pallas_call(
        functools.partial(corners_kernel, cap, vregs),
        out_shape=jax.ShapeDtypeStruct((frames, slot.shape[1]), jnp.float32),
        in_specs=[vmem] * 4,
        out_specs=vmem,
        scratch_shapes=[
            pltpu.VMEM((entries * (frames + 1), LANES), jnp.bfloat16),
            pltpu.VMEM((entries, LANES), jnp.float32),
        ],
        compiler_params=pltpu.CompilerParams(vmem_limit_bytes=24 * 2 ** 20),
        name="corners",
    )(vals.reshape(n * message, LANES), area_at, slot, bary)


def solution(mesh):
    placed = (
        P("tm", "slab"),
        P(None, "slab"),
        P(("slab", "tm"), None, None),
        P("slab"),
        P("slab", None, None),
        P(None, "slab"),
        P(None, "slab"),
    )
    return jax.shard_map(
        shards, mesh=mesh, in_specs=placed, out_specs=P("tm", "slab"), check_vma=False
    )
```

time: 38.2 us -> 26.9 us (0.70)
  Pallas kernels: 34.5 us -> 24.8 us
  local copies, waits for them, and re-layouts: 3.37 us -> 1.77 us
    pallas_call x1, Pallas kernels: 15.8 us -> 4.89 us  [shards(): pl.pallas_call(functools.partial(corners_kernel, cap, vregs), out_shape=j...]
    pallas_call x1, Pallas kernels: 18.7 us -> 19.9 us  [shards(): pl.pallas_call(functools.partial(exchange_kernel, n, m, vregs), out_shape...]
    reshape x2 -> x0, local copies, waits for them, and re-layouts: 0.84 us -> none  [the longest x1 0.82 us: shards(): slot.reshape(rows, LANES)]
    unnamed x12 -> x8, local copies, waits for them, and re-layouts: 2.53 us -> 1.77 us
where the time goes in v2:
time: 26.9 us; the launch traced here: 26.6 us
  Pallas kernels  24.8 us (92%)
  local copies, waits for them, and re-layouts  1.77 us (7%)
    pallas_call x1, Pallas kernels, shards(): pl.pallas_call(functools.partial(exchange_kernel, n, m, vregs), out_shape...  19.9 us
    pallas_call x1, Pallas kernels, shards(): pl.pallas_call(functools.partial(corners_kernel, cap, vregs), out_shape=j...  4.89 us
    unnamed x8, local copies, waits for them, and re-layouts  1.77 us

profile of v2, /device:TPU:0, one launch (start us, length us, event | category | flops | bytes accessed | tf_op | source)
XLA Modules:
  0.0 26.6 jit_solution(16381323451851287012)
XLA Ops:
  0.0 0.0 copy-start.2
  0.0 0.0 copy-start.3
  0.0 19.9 %exchange.1 = (bf16[16,48,128]{2,1,0:T(8,128)(2,1)}, f32[16,8,128]{2,1,0:T(8,128)}) custom-call(s32[2,16]{1,0:T(2,128)} %tidx.1, bf16[8,16384]{1,0:T(8,128)(2,1)} %bold_in.1, bf16[8,256,128]{2,1,0:T(8,128)(2,1)} %w.1, bf16[16,128]{1,0:T(8,128)(2,1)} %bitcast.5, s32[16,768]{1,0:T(8,128)} %bitcast.4), custom_call_target="tpu_custom_call" | custom-call | tf_op jit(solution)/shard_map/exchange/pallas_call | solution.py:275
  19.9 0.0 copy-done.2
  19.9 0.0 copy-done.3
  19.9 0.0 copy-start
  20.0 0.9 %copy-done = bf16[16,48,128]{2,1,0:T(8,128)(2,1)S(1)} copy-done((bf16[16,48,128]{2,1,0:T(8,128)(2,1)S(1)}, bf16[16,48,128]{2,1,0:T(8,128)(2,1)}, u32[]{:S(2)}) %copy-start) | copy-done | bytes 196632
  20.9 0.0 copy-start.1
  20.9 0.8 %copy-done.1 = f32[16,8,128]{2,1,0:T(8,128)S(1)} copy-done((f32[16,8,128]{2,1,0:T(8,128)S(1)}, f32[16,8,128]{2,1,0:T(8,128)}, u32[]{:S(2)}) %copy-start.1) | copy-done | bytes 65560
  21.7 4.9 %corners.1 = f32[8,2048]{1,0:T(8,128)} custom-call(bf16[768,128]{1,0:T(8,128)(2,1)S(1)} %bitcast.3, f32[16,8,128]{2,1,0:T(8,128)S(1)} %copy-done.1, s32[3,2048]{1,0:T(4,128)S(1)} %copy-done.2, f32[3,2048]{1,0:T(4,128)S(1)} %copy-done.3), custom_call_target="tpu_custom_call" | custom-call | tf_op jit(solution)/shard_map/corners/pallas_call | solution.py:299
Async XLA Ops:
  0.0 19.9 %copy-start.2 = (s32[3,2048]{1,0:T(4,128)S(1)}, s32[3,2048]{1,0:T(4,128)}, u32[]{:S(2)}) copy-start(s32[3,2048]{1,0:T(4,128)} %slot.1) | copy-start | bytes 73732
  0.0 19.9 %copy-start.3 = (f32[3,2048]{1,0:T(4,128)S(1)}, f32[3,2048]{1,0:T(4,128)}, u32[]{:S(2)}) copy-start(f32[3,2048]{1,0:T(4,128)} %bary.1) | copy-start | bytes 73732
  19.9 0.9 %copy-start = (bf16[16,48,128]{2,1,0:T(8,128)(2,1)S(1)}, bf16[16,48,128]{2,1,0:T(8,128)(2,1)}, u32[]{:S(2)}) copy-start(bf16[16,48,128]{2,1,0:T(8,128)(2,1)} %get-tuple-element.7) | copy-start | bytes 589828
  20.9 0.8 %copy-start.1 = (f32[16,8,128]{2,1,0:T(8,128)S(1)}, f32[16,8,128]{2,1,0:T(8,128)}, u32[]{:S(2)}) copy-start(f32[16,8,128]{2,1,0:T(8,128)} %get-tuple-element.8.area_at) | copy-start | bytes 196612

commit v3 on v2

--- a/solution.py
+++ b/solution.py
@@ -8,6 +8,7 @@
 from jax.sharding import PartitionSpec as P
 
 HALO_T = 8
+GROUP = 4
 LANES = 128
 MESH = pl.DeviceIdType.MESH
 
@@ -21,8 +22,8 @@
     return jnp.where(rows == lo, 1.0, 0.0).astype(jnp.bfloat16)
 
 
-def exchange_kernel(n, m, vregs, tidx, bold_in, w, area, wanted_in, vals, area_at, ext, wall, nat, req, rq, areas, out_buf,
-                    bold, wanted, in_s, halo_s, halo_r, w_s, w_r, rq_s, rq_r, ar_s, ar_r, va_s, va_r):
+def exchange_kernel(n, m, vregs, tidx, bold_in, w, area, wanted_in, slot_in, bary_in, out, vals, area_at, ext, wall, nat,
+                    req, rq, areas, out_buf, bold, wanted, slot, bary, tbl, packed, in_s, halo_s, halo_r, w_s, w_r, rq_s, rq_r, ar_s, ar_r, va_s, va_r):
     me = lax.axis_index("slab")
     t = lax.axis_index("tm")
     tiles = bold.shape[1] // LANES
@@ -37,10 +38,14 @@
     load_wanted = pltpu.make_async_copy(wanted_in, wanted, in_s.at[1])
     load_area = pltpu.make_async_copy(area, areas.at[me], in_s.at[2])
     mine = pltpu.make_async_copy(w, wall.at[pl.ds(t * own, own)], w_s.at[0])
+    load_slot = pltpu.make_async_copy(slot_in, slot, in_s.at[3])
+    load_bary = pltpu.make_async_copy(bary_in, bary, in_s.at[4])
     load_bold.start()
     load_wanted.start()
     load_area.start()
     mine.start()
+    load_slot.start()
+    load_bary.start()
     barrier = pltpu.get_barrier_semaphore()
 
     @pl.loop(1, n)
@@ -160,21 +165,33 @@
                 acc = jnp.where(hi == h, found[h * frames:(h + 1) * frames], acc)
             put(v, jnp.concatenate([acc[:, :LANES], acc[:, LANES:]], axis=0).astype(jnp.bfloat16))
 
-    @pl.loop(1, n)
-    def _(r):
-        to = lax.rem(me + r, n)
-        request_copy(n - r, to, to).wait_recv()
-
-        def put(v, piece):
-            out_buf[to, v * 16:(v + 1) * 16, :] = piece
-
-        selected(rq[to], put)
-        value_copy(r, to, me).start()
-
-    def put_own(v, piece):
-        vals[me, v * 16:(v + 1) * 16, :] = piece
-
-    selected(req[me], put_own)
+    rq[me] = req[me]
+
+    @pl.loop(0, n // GROUP)
+    def _(u):
+        for j in range(GROUP):
+            r = u * GROUP + j + 1
+
+            @pl.when(r < n)
+            def _():
+                to = lax.rem(me + r, n)
+                request_copy(n - r, to, to).wait_recv()
+
+        for j in range(GROUP):
+            to = lax.rem(me + u * GROUP + j + 1, n)
+
+            def put(v, piece):
+                out_buf[to, v * 16:(v + 1) * 16, :] = piece
+
+            selected(rq[to], put)
+        for j in range(GROUP):
+            r = u * GROUP + j + 1
+
+            @pl.when(r < n)
+            def _():
+                value_copy(r, lax.rem(me + r, n), me).start()
+
+    vals[me] = out_buf[me]
 
     @pl.loop(1, n)
     def _(r):
@@ -191,10 +208,15 @@
             acc = jnp.where(hi == h, pick(jnp.broadcast_to(a[h:h + 1], (8, LANES)), lo), acc)
         area_at[s] = acc
 
+    load_slot.wait()
+    load_bary.wait()
+
     @pl.loop(1, n)
     def _(r):
         source = lax.rem(me + n - r, n)
         value_copy(r, source, source).wait_recv()
+
+    corners(cap, vregs, vals, area_at, slot, bary, out, tbl, packed)
 
     @pl.loop(1, n)
     def _(r):
@@ -215,13 +237,13 @@
         to_left.wait_send()
 
 
-def corners_kernel(cap, vregs, vals, area_at, slot, bary, out, tbl, packed):
+def corners(cap, vregs, vals, area_at, slot, bary, out, tbl, packed):
     n = area_at.shape[0]
     half = vregs // 2
     frames = out.shape[0]
     entries = n * vregs
     width = 2 * LANES
-    tbl[:entries * frames] = vals[...]
+    tbl[:entries * frames] = vals[...].reshape(entries * frames, LANES)
     for s in range(n):
         packed[s * vregs:(s + 1) * vregs] = area_at[s, :vregs]
     tbl[entries * frames:] = packed[...].astype(jnp.bfloat16)
@@ -272,15 +294,14 @@
     hbm = pl.BlockSpec(memory_space=pltpu.HBM)
     smem = pl.BlockSpec(memory_space=pltpu.SMEM)
     sem = lambda k: pltpu.SemaphoreType.DMA((k,))
-    vals, area_at = pl.pallas_call(
+    return pl.pallas_call(
         functools.partial(exchange_kernel, n, m, vregs),
-        out_shape=(
-            jax.ShapeDtypeStruct((n, message, LANES), jnp.bfloat16),
-            jax.ShapeDtypeStruct((n, 8, LANES), jnp.float32),
-        ),
-        in_specs=[smem, hbm, hbm, hbm, hbm],
-        out_specs=(vmem, vmem),
+        out_shape=jax.ShapeDtypeStruct((frames, slot.shape[1]), jnp.float32),
+        in_specs=[smem] + [hbm] * 6,
+        out_specs=vmem,
         scratch_shapes=[
+            pltpu.VMEM((n, message, LANES), jnp.bfloat16),
+            pltpu.VMEM((n, 8, LANES), jnp.float32),
             pltpu.VMEM((bold.shape[1] // LANES + 2 * HALO_T, frames, LANES), jnp.float32),
             pltpu.VMEM((blocks, depth, tile), jnp.bfloat16),
             pltpu.VMEM((blocks, frames, LANES), jnp.float32),
@@ -290,24 +311,16 @@
             pltpu.VMEM((n, message, LANES), jnp.bfloat16),
             pltpu.VMEM(bold.shape, jnp.bfloat16),
             pltpu.VMEM((n, cap), jnp.int32),
-            sem(3), sem(2), sem(2), sem(m), sem(m), sem(n), sem(n), sem(n), sem(n), sem(n), sem(n),
+            pltpu.VMEM(slot.shape, jnp.int32),
+            pltpu.VMEM(bary.shape, jnp.float32),
+            pltpu.VMEM((entries * (frames + 1), LANES), jnp.bfloat16),
+            pltpu.VMEM((entries, LANES), jnp.float32),
+            sem(5), sem(2), sem(2), sem(m), sem(m), sem(n), sem(n), sem(n), sem(n), sem(n), sem(n),
         ],
         compiler_params=pltpu.CompilerParams(
             collective_id=0, has_side_effects=True),
         name="exchange",
-    )(tile_index, bold, weights, area.reshape(-1, LANES), requests.reshape(n, cap))
-    return pl.pallas_call(
-        functools.partial(corners_kernel, cap, vregs),
-        out_shape=jax.ShapeDtypeStruct((frames, slot.shape[1]), jnp.float32),
-        in_specs=[vmem] * 4,
-        out_specs=vmem,
-        scratch_shapes=[
-            pltpu.VMEM((entries * (frames + 1), LANES), jnp.bfloat16),
-            pltpu.VMEM((entries, LANES), jnp.float32),
-        ],
-        compiler_params=pltpu.CompilerParams(vmem_limit_bytes=24 * 2 ** 20),
-        name="corners",
-    )(vals.reshape(n * message, LANES), area_at, slot, bary)
+    )(tile_index, bold, weights, area.reshape(-1, LANES), requests.reshape(n, cap), slot, bary)
 
 
 def solution(mesh):

time: 26.9 us -> 25.2 us (0.937)
  Pallas kernels: 24.8 us -> 23.5 us
  local copies, waits for them, and re-layouts: 1.77 us -> 1.47 us
    pallas_call x1 -> x0, Pallas kernels: 4.89 us -> none  [shards(): pl.pallas_call(functools.partial(corners_kernel, cap, vregs), out_shape=j...]
    pallas_call x1, Pallas kernels: 19.9 us -> 23.5 us  [shards(): pl.pallas_call(functools.partial(exchange_kernel, n, m, vregs), out_shape...]
    unnamed x8 -> x1, local copies, waits for them, and re-layouts: 1.77 us -> 1.47 us
where the time goes in v3:
time: 25.2 us; the launch traced here: 25 us
  Pallas kernels  23.5 us (93%)
  local copies, waits for them, and re-layouts  1.47 us (6%)
    pallas_call x1, Pallas kernels, shards(): pl.pallas_call(functools.partial(exchange_kernel, n, m, vregs), out_shape...  23.5 us
    unnamed x1, local copies, waits for them, and re-layouts  1.47 us

profile of v3, /device:TPU:0, one launch (start us, length us, event | category | flops | bytes accessed | tf_op | source)
XLA Modules:
  0.0 25.0 jit_solution(16453951748804711120)
XLA Ops:
  0.0 23.5 %exchange.1 = f32[8,2048]{1,0:T(8,128)} custom-call(s32[2,16]{1,0:T(2,128)} %tidx.1, bf16[8,16384]{1,0:T(8,128)(2,1)} %bold_in.1, bf16[8,256,128]{2,1,0:T(8,128)(2,1)} %w.1, bf16[16,128]{1,0:T(8,128)(2,1)} %bitcast.3, s32[16,768]{1,0:T(8,128)} %bitcast.2, s32[3,2048]{1,0:T(4,128)} %slot_in.1, f32[3,2048]{1,0:T(4,128)} %bary_in.1), custom_call_target="tpu_custom_call" | custom-call | tf_op jit(solution)/shard_map/exchange/pallas_call | solution.py:297
  23.5 1.5 %copy.9 = f32[8,2048]{1,0:T(8,128)} copy(f32[8,2048]{1,0:T(8,128)} %exchange.1) | data formatting | bytes 131072

commit v4 on v3

--- a/solution.py
+++ b/solution.py
@@ -17,8 +17,8 @@
     return jnp.take_along_axis(table, lanes, axis=1, mode="promise_in_bounds")
 
 
-def one_hot(lo):
-    rows = lax.broadcasted_iota(jnp.int32, (LANES, lo.shape[1]), 0)
+def one_hot(lo, depth=LANES):
+    rows = lax.broadcasted_iota(jnp.int32, (depth, lo.shape[1]), 0)
     return jnp.where(rows == lo, 1.0, 0.0).astype(jnp.bfloat16)
 
 
@@ -243,10 +243,14 @@
     frames = out.shape[0]
     entries = n * vregs
     width = 2 * LANES
-    tbl[:entries * frames] = vals[...].reshape(entries * frames, LANES)
+    part = entries // 2
+    top_rows = part * frames
+    tbl[:top_rows, :LANES] = vals[:n // 2].reshape(top_rows, LANES)
+    tbl[:top_rows, LANES:] = vals[n // 2:].reshape(top_rows, LANES)
     for s in range(n):
         packed[s * vregs:(s + 1) * vregs] = area_at[s, :vregs]
-    tbl[entries * frames:] = packed[...].astype(jnp.bfloat16)
+    tbl[top_rows:, :LANES] = packed[:part].astype(jnp.bfloat16)
+    tbl[top_rows:, LANES:] = packed[part:].astype(jnp.bfloat16)
 
     @pl.loop(0, out.shape[1] // width)
     def _(g):
@@ -261,10 +265,13 @@
                 source = ((flat.astype(jnp.float32) + 0.5) * (1.0 / cap)).astype(jnp.int32)
                 rest = flat - source * cap
                 lo, hi = rest & (LANES - 1), source * vregs + (rest >> 7)
-            found = jnp.dot(tbl[...], one_hot(lo), preferred_element_type=jnp.float32)
+            late = hi >= part
+            lo = jnp.where(late, lo + LANES, lo)
+            hi = jnp.where(late, hi - part, hi)
+            found = jnp.dot(tbl[...], one_hot(lo, width), preferred_element_type=jnp.float32)
             wide = jnp.broadcast_to(hi, (frames, width))
             acc = jnp.zeros((frames, width), jnp.float32)
-            for s in range(n):
+            for s in range(n // 2):
                 for v in range(half):
                     for j in range(2):
                         e = (s * half + v) * 2 + j
@@ -272,8 +279,8 @@
                         acc = jnp.where(wide == s * vregs + j * half + v, here, acc)
             row8 = lax.broadcasted_iota(jnp.int32, (8, width), 0)
             spread = jnp.zeros((8, width), jnp.float32)
-            for b in range(entries // 8):
-                at8 = entries * frames + b * 8
+            for b in range(part // 8):
+                at8 = top_rows + b * 8
                 spread = jnp.where(wide == row8 + b * 8, found[at8:at8 + 8], spread)
             factor = bary[k:k + 1, at] * jnp.sum(spread, axis=0, keepdims=True)
             top = top + factor * acc
@@ -313,7 +320,7 @@
             pltpu.VMEM((n, cap), jnp.int32),
             pltpu.VMEM(slot.shape, jnp.int32),
             pltpu.VMEM(bary.shape, jnp.float32),
-            pltpu.VMEM((entries * (frames + 1), LANES), jnp.bfloat16),
+            pltpu.VMEM((entries // 2 * (frames + 1), 2 * LANES), jnp.bfloat16),
             pltpu.VMEM((entries, LANES), jnp.float32),
             sem(5), sem(2), sem(2), sem(m), sem(m), sem(n), sem(n), sem(n), sem(n), sem(n), sem(n),
         ],

time: 25.2 us -> 24.2 us (0.960)
  Pallas kernels: 23.5 us -> 22.5 us
    pallas_call x1, Pallas kernels: 23.5 us -> 22.5 us  [shards(): pl.pallas_call(functools.partial(exchange_kernel, n, m, vregs), out_shape...]
where the time goes in v4:
time: 24.2 us; the launch traced here: 24 us
  Pallas kernels  22.5 us (93%)
  local copies, waits for them, and re-layouts  1.47 us (6%)
    pallas_call x1, Pallas kernels, shards(): pl.pallas_call(functools.partial(exchange_kernel, n, m, vregs), out_shape...  22.5 us
    unnamed x1, local copies, waits for them, and re-layouts  1.47 us

profile of v4, /device:TPU:0, one launch (start us, length us, event | category | flops | bytes accessed | tf_op | source)
XLA Modules:
  0.0 24.0 jit_solution(16384461561515951115)
XLA Ops:
  0.0 22.5 %exchange.1 = f32[8,2048]{1,0:T(8,128)} custom-call(s32[2,16]{1,0:T(2,128)} %tidx.1, bf16[8,16384]{1,0:T(8,128)(2,1)} %bold_in.1, bf16[8,256,128]{2,1,0:T(8,128)(2,1)} %w.1, bf16[16,128]{1,0:T(8,128)(2,1)} %bitcast.3, s32[16,768]{1,0:T(8,128)} %bitcast.2, s32[3,2048]{1,0:T(4,128)} %slot_in.1, f32[3,2048]{1,0:T(4,128)} %bary_in.1), custom_call_target="tpu_custom_call" | custom-call | tf_op jit(solution)/shard_map/exchange/pallas_call | solution.py:304
  22.5 1.5 %copy.9 = f32[8,2048]{1,0:T(8,128)} copy(f32[8,2048]{1,0:T(8,128)} %exchange.1) | data formatting | bytes 131072

commit v5 on v4

--- a/solution.py
+++ b/solution.py
@@ -152,16 +152,22 @@
             x = jnp.concatenate([ext[tidx[k, block]] for k in range(2)], axis=1).astype(jnp.bfloat16)
             nat[block] = jnp.dot(x, wall[block], preferred_element_type=jnp.float32)
 
-    table = nat[...].reshape(blocks * frames, LANES).astype(jnp.bfloat16)
+    part = blocks // 2
+    table = jnp.concatenate(
+        [nat[:part].reshape(part * frames, LANES), nat[part:].reshape(part * frames, LANES)], axis=1
+    ).astype(jnp.bfloat16)
 
     def selected(rows, put):
         for v in range(half):
             row = jnp.concatenate([rows[v:v + 1], rows[half + v:half + v + 1]], axis=1)
             lo = row & (LANES - 1)
-            hi = jnp.broadcast_to(row >> 7, (frames, 2 * LANES))
-            found = jnp.dot(table, one_hot(lo), preferred_element_type=jnp.float32)
+            hi = row >> 7
+            late = hi >= part
+            lo = jnp.where(late, lo + LANES, lo)
+            hi = jnp.broadcast_to(jnp.where(late, hi - part, hi), (frames, 2 * LANES))
+            found = jnp.dot(table, one_hot(lo, 2 * LANES), preferred_element_type=jnp.float32)
             acc = found[:frames]
-            for h in range(1, blocks):
+            for h in range(1, part):
                 acc = jnp.where(hi == h, found[h * frames:(h + 1) * frames], acc)
             put(v, jnp.concatenate([acc[:, :LANES], acc[:, LANES:]], axis=0).astype(jnp.bfloat16))
 
@@ -252,7 +258,7 @@
     tbl[top_rows:, :LANES] = packed[:part].astype(jnp.bfloat16)
     tbl[top_rows:, LANES:] = packed[part:].astype(jnp.bfloat16)
 
-    @pl.loop(0, out.shape[1] // width)
+    @pl.loop(0, out.shape[1] // width, unroll=2)
     def _(g):
         at = pl.ds(pl.multiple_of(g * width, width), width)
         top = jnp.zeros((frames, width), jnp.float32)

time: 24.2 us -> 23.2 us (0.959)
  Pallas kernels: 22.5 us -> 21.6 us
    pallas_call x1, Pallas kernels: 22.5 us -> 21.6 us  [shards(): pl.pallas_call(functools.partial(exchange_kernel, n, m, vregs), out_shape...]
where the time goes in v5:
time: 23.2 us; the launch traced here: 23.1 us
  Pallas kernels  21.6 us (93%)
  local copies, waits for them, and re-layouts  1.47 us (6%)
    pallas_call x1, Pallas kernels, shards(): pl.pallas_call(functools.partial(exchange_kernel, n, m, vregs), out_shape...  21.6 us
    unnamed x1, local copies, waits for them, and re-layouts  1.47 us

profile of v5, /device:TPU:0, one launch (start us, length us, event | category | flops | bytes accessed | tf_op | source)
XLA Modules:
  0.0 23.1 jit_solution(3728192809954450208)
XLA Ops:
  0.0 21.6 %exchange.1 = f32[8,2048]{1,0:T(8,128)} custom-call(s32[2,16]{1,0:T(2,128)} %tidx.1, bf16[8,16384]{1,0:T(8,128)(2,1)} %bold_in.1, bf16[8,256,128]{2,1,0:T(8,128)(2,1)} %w.1, bf16[16,128]{1,0:T(8,128)(2,1)} %bitcast.3, s32[16,768]{1,0:T(8,128)} %bitcast.2, s32[3,2048]{1,0:T(4,128)} %slot_in.1, f32[3,2048]{1,0:T(4,128)} %bary_in.1), custom_call_target="tpu_custom_call" | custom-call | tf_op jit(solution)/shard_map/exchange/pallas_call | solution.py:310
  21.6 1.5 %copy.9 = f32[8,2048]{1,0:T(8,128)} copy(f32[8,2048]{1,0:T(8,128)} %exchange.1) | data formatting | bytes 131072
